TPU v7x, 512 devices: a whole 4x8x8 slice. The times are simulated.
512 devices in a mesh: train: 16 (over x, z_hi, core), roll: 32 (over z_lo, y).
Axes of the slice: x: 4, y: 8, z: 8 (z_hi: 2, z_lo: 4; z = z_hi * 4 + z_lo), core: 2. Of those that a mesh axis runs over, the one named last changes fastest.
Arguments:
- hidden: bfloat16 [24576, 8192], P(('train', 'roll')), may hold values from -6 to 6
- ssm_state: bfloat16 [24576, 1, 64, 256], P(('train', 'roll')), may hold values from -6 to 6
- conv_state: bfloat16 [24576, 3, 576], P(('train', 'roll')), may hold values from -6 to 6
- lengths: int32 [24576], P(('train', 'roll')), may hold values from 1 to 8
- dest_owner: int32 [24576], P(('train', 'roll')), may hold values from 0 to 31, as said below
- dest_slot: int32 [24576], P(('train', 'roll')), may hold values from 0 to 47, as said below
- weights_in: bfloat16 [8192, 640], P('train'), may hold values from -0.0625 to 0.0625
- weights_dt: bfloat16 [8192, 1], P('train'), may hold values from -0.0625 to 0.0625
- weights_out: bfloat16 [64, 8192], P(None, 'train'), may hold values from -0.75 to 0.75
- input_gain: float32 [8192], replicated, may hold values from 0.5 to 1.5
- conv_weight: float32 [4, 576], replicated, may hold values from -3 to 3
- conv_bias: float32 [576], replicated, may hold values from -3 to 3
- delta_bias: float32 [1], replicated, may hold values from -3 to 1
- decay_log: float32 [1], replicated, may hold values from -1 to 1.5
- skip_gain: float32 [1], replicated, may hold values from 0.5 to 1.5
- output_gain: float32 [64], replicated, may hold values from 0.5 to 1.5
Outputs:
- moved_state: bfloat16 [24576, 1, 64, 256], P(('train', 'roll'))
- moved_conv: bfloat16 [24576, 3, 576], P(('train', 'roll'))
Inputs may be any that keep to these rules, and one draw needn't show every extreme that they name: `dest_owner`: within one train index, each row names a roll index as its new owner. A device sends at most 2 rows to one owner, and exactly 2 to some owner. `dest_slot`: within one train index, each owner's 48 slots are each named by exactly one row.
All inputs are finite; a program needn't handle non-finite values.
Results may differ from a plain program's by a relative error of at most 0.015.
Values may be sent and summed in bfloat16 or wider, within the bound.
No kernel may reach another device: no remote copies, remote signals or barrier semaphores. Data moves between devices by JAX's collectives and lax.ppermute only.
A program may use at most 64 MiB of HBM per device.

v0:
```python
import jax
import jax.numpy as jnp
from jax import lax
from jax.sharding import PartitionSpec as P

STEPS = 4


def rms_scale(values, gain):
    return values * lax.rsqrt(jnp.mean(values * values, axis=-1, keepdims=True) + 1e-05) * gain


def decode_steps(
    hidden,
    ssm_state,
    conv_state,
    lengths,
    weights_in,
    weights_dt,
    weights_out,
    input_gain,
    conv_weight,
    conv_bias,
    delta_bias,
    decay_log,
    skip_gain,
    output_gain,
):
    inner = weights_out.shape[0]
    heads = delta_bias.shape[0]
    head_size = inner // heads
    nstate = ssm_state.shape[-1]
    count = hidden.shape[0]
    for step in range(STEPS):
        live = lengths > step
        current = hidden.astype(jnp.float32)
        normed = rms_scale(current, input_gain).astype(jnp.bfloat16)
        projected = jnp.dot(normed, weights_in, preferred_element_type=jnp.float32)
        delta_raw = jnp.dot(normed, weights_dt, preferred_element_type=jnp.float32)
        gate_part = projected[:, :inner]
        conv_input = projected[:, inner:].astype(jnp.bfloat16)
        window = jnp.concatenate([conv_state, conv_input[:, None, :]], axis=1)
        mixed = jax.nn.silu(
            jnp.sum(window.astype(jnp.float32) * conv_weight[None], axis=1) + conv_bias
        )
        inputs_x = mixed[:, :inner].reshape(count, heads, head_size)
        input_b = mixed[:, inner : inner + nstate]
        output_c = mixed[:, inner + nstate :]
        delta = jax.nn.softplus(delta_raw + delta_bias)
        decay = jnp.exp(-delta * jnp.exp(decay_log))
        updated = (
            ssm_state.astype(jnp.float32) * decay[:, :, None, None]
            + (delta[:, :, None] * inputs_x)[:, :, :, None] * input_b[:, None, None, :]
        )
        readout = (
            jnp.sum(updated * output_c[:, None, None, :], axis=-1)
            + skip_gain[None, :, None] * inputs_x
        )
        gated = readout.reshape(count, inner) * jax.nn.silu(gate_part)
        normed_out = rms_scale(gated, output_gain).astype(jnp.bfloat16)
        layer_out = jnp.dot(normed_out, weights_out, preferred_element_type=jnp.float32)
        next_hidden = (current + layer_out).astype(jnp.bfloat16)
        ssm_state = jnp.where(live[:, None, None, None], updated.astype(jnp.bfloat16), ssm_state)
        conv_state = jnp.where(live[:, None, None], window[:, 1:], conv_state)
        hidden = jnp.where(live[:, None], next_hidden, hidden)
    return (ssm_state, conv_state)


def body(
    hidden,
    ssm_state,
    conv_state,
    lengths,
    dest_owner,
    dest_slot,
    weights_in,
    weights_dt,
    weights_out,
    input_gain,
    conv_weight,
    conv_bias,
    delta_bias,
    decay_log,
    skip_gain,
    output_gain,
):
    members = lax.axis_size("roll")
    full_in, full_dt, full_out = (
        lax.all_gather(weights_in, "train", axis=0, tiled=True),
        lax.all_gather(weights_dt, "train", axis=0, tiled=True),
        lax.all_gather(weights_out, "train", axis=1, tiled=True),
    )
    new_state, new_conv = decode_steps(
        hidden,
        ssm_state,
        conv_state,
        lengths,
        full_in,
        full_dt,
        full_out,
        input_gain,
        conv_weight,
        conv_bias,
        delta_bias,
        decay_log,
        skip_gain,
        output_gain,
    )
    rows = hidden.shape[0]
    capacity = max(2, rows // members + 1)
    slots = members * capacity
    unfinished = lengths > STEPS
    order = jnp.arange(rows)
    earlier = (dest_owner[:, None] == dest_owner[None, :]) & (order[None, :] < order[:, None])
    rank = jnp.sum(earlier.astype(jnp.int32), axis=1)
    place = dest_owner * capacity + rank
    picker = (jnp.arange(slots)[:, None] == place[None, :]).astype(jnp.bfloat16)
    kept_state = jnp.where(
        unfinished[:, None, None, None], new_state, jnp.zeros_like(new_state)
    ).reshape(rows, -1)
    kept_conv = jnp.where(unfinished[:, None, None], new_conv, jnp.zeros_like(new_conv)).reshape(
        rows, -1
    )
    codes = jnp.where(unfinished, dest_slot + 1, 0).astype(jnp.bfloat16)
    send_state = (
        jnp.dot(picker, kept_state, preferred_element_type=jnp.float32)
        .astype(jnp.bfloat16)
        .reshape(members, capacity, -1)
    )
    send_conv = (
        jnp.dot(picker, kept_conv, preferred_element_type=jnp.float32)
        .astype(jnp.bfloat16)
        .reshape(members, capacity, -1)
    )
    send_code = (
        jnp.dot(picker, codes, preferred_element_type=jnp.float32)
        .astype(jnp.bfloat16)
        .reshape(members, capacity)
    )
    got_state, got_conv, got_code = (
        lax.all_to_all(send_state, "roll", split_axis=0, concat_axis=0, tiled=True),
        lax.all_to_all(send_conv, "roll", split_axis=0, concat_axis=0, tiled=True),
        lax.all_to_all(send_code, "roll", split_axis=0, concat_axis=0, tiled=True),
    )
    wanted = (jnp.arange(rows) + 1).astype(jnp.bfloat16)
    target = (got_code.reshape(-1)[None, :] == wanted[:, None]).astype(jnp.bfloat16)
    moved_state = (
        jnp.dot(target, got_state.reshape(slots, -1), preferred_element_type=jnp.float32)
        .astype(jnp.bfloat16)
        .reshape(new_state.shape)
    )
    moved_conv = (
        jnp.dot(target, got_conv.reshape(slots, -1), preferred_element_type=jnp.float32)
        .astype(jnp.bfloat16)
        .reshape(new_conv.shape)
    )
    return (moved_state, moved_conv)


def solution(mesh):
    return jax.shard_map(
        body,
        mesh=mesh,
        in_specs=(
            P(("train", "roll"), None),
            P(("train", "roll"), None, None, None),
            P(("train", "roll"), None, None),
            P(("train", "roll")),
            P(("train", "roll")),
            P(("train", "roll")),
            P("train", None),
            P("train", None),
            P(None, "train"),
            P(),
            P(),
            P(),
            P(),
            P(),
            P(),
            P(),
        ),
        out_specs=(P(("train", "roll"), None, None, None), P(("train", "roll"), None, None)),
        check_vma=False,
    )
```

profile of v0, /device:TPU:24, one launch (start us, length us, event | category | flops | bytes accessed | tf_op | source)
XLA Modules:
  0.0 320.5 jit_solution(5175397795754622397)
XLA Ops:
  7.9 0.9 convert_reduce_fusion
  11.0 12.9 %all-to-all-start = ((bf16[32,1,2]{2,1,0:T(2,128)(2,1)}), bf16[32,1,2]{2,1,0:T(2,128)(2,1)S(1)}, u32[]{:S(2)}, u32[]{:S(2)}) async-start(bf16[32,1,2]{2,1,0:T(2,128)(2,1)} %all_to_all.16), calls=%async_computation | async-start | bytes 32768 | tf_op jit(solution)/shard_map/all_to_all | solution.py:143
  27.4 1.4 fusion.14
  28.8 38.1 %all_gather.9 = bf16[8192,1]{0,1:T(2,128)(2,1)S(1)} all-gather(bf16[512,1]{0,1:T(2,128)(2,1)S(1)} %copy-done.7), channel_id=1, replica_groups=mesh['train'=16,'roll'=32] {'train'}, dimensions={0}, use_global_device_ids=true | all-gather | bytes 17408 | tf_op jit(solution)/shard_map/all_gather | solution.py:90
  67.3 79.3 %all-gather.3.cloned.1.call-done = bf16[8192,640]{1,0:T(8,128)(2,1)} async-done(((bf16[512,640]{1,0:T(8,128)(2,1)}), bf16[8192,640]{1,0:T(8,128)(2,1)}) %all-gather.3.cloned.1.call-update) | async-done | bytes 10485776 | tf_op jit(solution)/shard_map/all_gather | solution.py:89
  146.6 6.0 %fusion.35 = f32[48,640]{1,0:T(8,128)S(1)} fusion(bf16[8192,640]{1,0:T(8,128)(2,1)} %all-gather.3.cloned.1.call-done, bf16[48,8192]{1,0:T(8,128)(2,1)S(1)} %copy-done.1, f32[8192]{0:T(1024)S(1)} %copy-done.2, f32[48]{0:T(128)S(1)} %add_rsqrt_fusion.6), kind=kOutput, calls=%fused_computation.74 | convolution fusion | flops 504889344 | bytes 11428032 | tf_op jit(solution)/shard_map/dot_general | solution.py:38
  153.1 1.7 multiply_reduce_fusion.2
  155.0 51.9 %all-gather.5.cloned.1.call-done = bf16[64,8192]{1,0:T(8,128)(2,1)} async-done(((bf16[64,512]{1,0:T(8,128)(2,1)}), bf16[64,8192]{1,0:T(8,128)(2,1)}) %all-gather.5.cloned.1.call-update) | async-done | bytes 1048592 | tf_op jit(solution)/shard_map/all_gather | solution.py:91
  206.9 1.9 fusion.17
  209.3 6.1 %fusion.32 = f32[48,640]{1,0:T(8,128)S(1)} fusion(bf16[8192,640]{1,0:T(8,128)(2,1)} %all-gather.3.cloned.1.call-done, bf16[48,8192]{1,0:T(8,128)(2,1)S(1)} %get-tuple-element.32, f32[48]{0:T(128)S(1)} %add_rsqrt_fusion.4, f32[8192]{0:T(1024)S(1)} %copy-done.2), kind=kOutput, calls=%fused_computation.73 | convolution fusion | flops 504889344 | bytes 11428032 | tf_op jit(solution)/shard_map/dot_general | solution.py:38
  215.9 2.8 multiply_reduce_fusion.1
  220.0 1.9 fusion.29
  222.4 2.9 multiply_reduce_fusion
  226.6 2.0 fusion.79
  230.3 7.8 %all-to-all-start.2 = ((bf16[32,2,1728]{2,1,0:T(2,128)(2,1)}), bf16[32,2,1728]{2,1,0:T(2,128)(2,1)S(1)}, u32[]{:S(2)}, u32[]{:S(2)}) async-start(bf16[32,2,1728]{2,1,0:T(2,128)(2,1)} %reshape.312), calls=%async_computation.2 | async-start | bytes 458752 | tf_op jit(solution)/shard_map/all_to_all | solution.py:142
  238.1 2.9 fusion.23
  241.0 0.9 copy.31
  242.7 2.7 reshape.308
  245.3 3.2 all-to-all-done.2
  248.5 6.9 %all-to-all-start.1 = ((bf16[32,2,16384]{2,1,0:T(2,128)(2,1)}), bf16[32,2,16384]{2,1,0:T(2,128)(2,1)S(1)}, u32[]{:S(2)}, u32[]{:S(2)}) async-start(bf16[32,2,16384]{2,1,0:T(2,128)(2,1)} %reshape.308), calls=%async_computation.1 | async-start | bytes 4194304 | tf_op jit(solution)/shard_map/all_to_all | solution.py:141
  256.9 50.8 %all-to-all-done.1 = bf16[32,2,16384]{2,1,0:T(2,128)(2,1)S(1)} async-done(((bf16[32,2,16384]{2,1,0:T(2,128)(2,1)}), bf16[32,2,16384]{2,1,0:T(2,128)(2,1)S(1)}, u32[]{:S(2)}, u32[]{:S(2)}) %all-to-all-start.1) | async-done | bytes 2097184 | tf_op jit(solution)/shard_map/all_to_all | solution.py:141
  307.8 2.2 reshape.309
  310.0 2.2 convolution_convert_fusion.1
  312.2 1.5 copy.32
  (86 shorter events, 12.9 us)
Async XLA Ops:
  7.2 59.7 %copy-start.1 = (bf16[48,8192]{1,0:T(8,128)(2,1)S(1)}, bf16[48,8192]{1,0:T(8,128)(2,1)}, u32[]{:S(2)}) copy-start(bf16[48,8192]{1,0:T(8,128)(2,1)} %param.16) | copy-start | bytes 2359300
  7.2 21.6 %copy-start.7 = (bf16[512,1]{0,1:T(2,128)(2,1)S(1)}, bf16[512,1]{0,1:T(2,128)(2,1)}, u32[]{:S(2)}) copy-start(bf16[512,1]{0,1:T(2,128)(2,1)} %param.23) | copy-start | bytes 3076
  7.2 59.7 %copy-start.2 = (f32[8192]{0:T(1024)S(1)}, f32[8192]{0:T(1024)}, u32[]{:S(2)}) copy-start(f32[8192]{0:T(1024)} %param.25) | copy-start | bytes 98308
  7.2 139.4 %all-gather.3.cloned.1.call-start = ((), (), s32[]{:S(2)}) async-start(), calls=%async_computation.3 | async-start | bytes 11141120 | tf_op jit(solution)/shard_map/all_gather | solution.py:89
  11.0 219.2 %all-to-all-start = ((bf16[32,1,2]{2,1,0:T(2,128)(2,1)}), bf16[32,1,2]{2,1,0:T(2,128)(2,1)S(1)}, u32[]{:S(2)}, u32[]{:S(2)}) async-start(bf16[32,1,2]{2,1,0:T(2,128)(2,1)} %all_to_all.16), calls=%async_computation | async-start | bytes 32768 | tf_op jit(solution)/shard_map/all_to_all | solution.py:143
  24.0 183.0 %all-gather.5.cloned.1.call-start = ((), (), s32[]{:S(2)}) async-start(), calls=%async_computation.4 | async-start | bytes 1114112 | tf_op jit(solution)/shard_map/all_gather | solution.py:91
  67.2 85.5 %copy-start.4 = (bf16[48,3,576]{2,0,1:T(8,128)(2,1)S(1)}, bf16[48,3,576]{2,0,1:T(8,128)(2,1)}, u32[]{:S(2)}) copy-start(bf16[48,3,576]{2,0,1:T(8,128)(2,1)} %param.18) | copy-start | bytes 497668
  67.3 85.5 %copy-start.5 = (f32[4,576]{1,0:T(4,128)S(1)}, f32[4,576]{1,0:T(4,128)}, u32[]{:S(2)}) copy-start(f32[4,576]{1,0:T(4,128)} %param.26) | copy-start | bytes 27652
  67.3 85.6 %copy-start.6 = (f32[576]{0:T(1024)S(1)}, f32[576]{0:T(1024)}, u32[]{:S(2)}) copy-start(f32[576]{0:T(1024)} %param.27) | copy-start | bytes 6916
  146.6 6.4 %copy-start = (bf16[48,1,64,256]{3,2,1,0:T(8,128)(2,1)S(1)}, bf16[48,1,64,256]{3,2,1,0:T(8,128)(2,1)}, u32[]{:S(2)}) copy-start(bf16[48,1,64,256]{3,2,1,0:T(8,128)(2,1)} %param.17) | copy-start | bytes 4718596
  152.8 54.2 %copy-start.8 = (f32[64]{0:T(128)S(1)}, f32[64]{0:T(128)}, u32[]{:S(2)}) copy-start(f32[64]{0:T(128)} %param.31) | copy-start | bytes 772
  208.8 11.2 %slice-start = ((s8[10485760]{0:T(1024)(128)(4,1)}), s8[4194304]{0:T(1024)(128)(4,1)S(1)}, s32[]{:S(2)}) async-start(s8[10485760]{0:T(1024)(128)(4,1)} %bitcast.73), calls=%async_computation.5 | async-start | bytes 8388608
  209.3 10.8 %slice-start.1 = ((s8[10485760]{0:T(1024)(128)(4,1)}), s8[4194304]{0:T(1024)(128)(4,1)S(1)}, s32[]{:S(2)}) async-start(s8[10485760]{0:T(1024)(128)(4,1)} %bitcast.73), calls=%async_computation.6 | async-start | bytes 8388608
  209.3 10.8 %slice-start.2 = ((s8[10485760]{0:T(1024)(128)(4,1)}), s8[2097152]{0:T(1024)(128)(4,1)S(1)}, s32[]{:S(2)}) async-start(s8[10485760]{0:T(1024)(128)(4,1)} %bitcast.73), calls=%async_computation.7 | async-start | bytes 4194304
  215.9 3.0 copy-start.3
  230.3 18.3 %all-to-all-start.2 = ((bf16[32,2,1728]{2,1,0:T(2,128)(2,1)}), bf16[32,2,1728]{2,1,0:T(2,128)(2,1)S(1)}, u32[]{:S(2)}, u32[]{:S(2)}) async-start(bf16[32,2,1728]{2,1,0:T(2,128)(2,1)} %reshape.312), calls=%async_computation.2 | async-start | bytes 458752 | tf_op jit(solution)/shard_map/all_to_all | solution.py:142
  248.5 59.2 %all-to-all-start.1 = ((bf16[32,2,16384]{2,1,0:T(2,128)(2,1)}), bf16[32,2,16384]{2,1,0:T(2,128)(2,1)S(1)}, u32[]{:S(2)}, u32[]{:S(2)}) async-start(bf16[32,2,16384]{2,1,0:T(2,128)(2,1)} %reshape.308), calls=%async_computation.1 | async-start | bytes 4194304 | tf_op jit(solution)/shard_map/all_to_all | solution.py:141
Sparse Core Ops, SparseCore 0:
  11.3 135.2 all-gather.2
  149.8 57.1 all-gather.4
where the time goes:
time: 321 us
  waiting for transfers between devices  187 us (58%)
  blocking collectives  38.1 us (12%)
  starting transfers between devices  27.7 us (9%)
  matrix products  25 us (8%)
  between operations  16.5 us (5%)
  other arithmetic  15.6 us (5%)
  local copies, waits for them, and re-layouts  11 us (3%)
    all_gather x1, waiting for transfers between devices, body(): lax.all_gather(weights_in, 'train', axis=0, tiled=True)  79.3 us
    all_gather x1, waiting for transfers between devices, body(): lax.all_gather(weights_out, 'train', axis=1, tiled=True)  51.9 us
    all_to_all x1, waiting for transfers between devices, body(): lax.all_to_all(send_state, 'roll', split_axis=0, concat_axis=0, tiled=True)  50.8 us
    all_gather x1, blocking collectives, body(): lax.all_gather(weights_dt, 'train', axis=0, tiled=True)  38.1 us
    dot_general x4, matrix products, decode_steps(): projected = jnp.dot(normed, weights_in, preferred_element_type=jnp.float32)  16 us
    all_to_all x1, starting transfers between devices, body(): lax.all_to_all(send_code, 'roll', split_axis=0, concat_axis=0, tiled=True)  12.9 us
    all_to_all x1, starting transfers between devices, body(): lax.all_to_all(send_conv, 'roll', split_axis=0, concat_axis=0, tiled=True)  7.81 us
    reduce_sum x3, other arithmetic, decode_steps(): jnp.sum(updated * output_c[:, None, None, :], axis=-1)  7.42 us
  transfers between devices with their start and end apart: 5, of which 4 were waited for; matrix products, arithmetic and copies ran while one was open for 14% of the time, Pallas kernels for 0%

commit v1 on v0

v1 whole, which is shorter than its diff:
```python
import functools

import jax
import jax.numpy as jnp
from jax import lax
from jax.experimental import pallas as pl
from jax.experimental.pallas import tpu as pltpu
from jax.sharding import PartitionSpec as P

STEPS = 4
CAP = 2
ROWS = 48
HEAD = 64
NS = 256
CONV = 576
WIDTH = 8192
NX = 4
NZ = 4
NY = 8
N_ROLL = NZ * NY
BLOCK = 512
SPAN = 4 * BLOCK
COLS = 768
GATE = CONV
BACK = GATE + HEAD
STEP = BACK + HEAD
LATE = NS + CONV + HEAD
F32 = jnp.float32
BF16 = jnp.bfloat16
VMEM = pl.BlockSpec(memory_space=pltpu.VMEM)
SMEM = pl.BlockSpec(memory_space=pltpu.SMEM)
HBM = pl.BlockSpec(memory_space=pltpu.HBM)


def prepare_kernel(
    owner_ref,
    state_ref,
    hidden_ref,
    gain_ref,
    in_ref,
    dt_ref,
    out_ref,
    send_ref,
    place_ref,
    weights_ref,
    square_ref,
    h0,
    h1,
    h2,
    h3,
    count_ref,
    states,
    rows,
    load_sem,
    state_sem,
    span_sem,
):
    train = lax.axis_index("train")
    load_rows = pltpu.make_async_copy(hidden_ref, rows, load_sem.at[0])
    load_rows.start()
    load_states = pltpu.make_async_copy(state_ref, states, load_sem.at[1])
    load_states.start()

    weights_ref[:, : 2 * NS] = in_ref[:, 2 * HEAD :]
    rest = in_ref[:, : 2 * HEAD].astype(F32)
    weights_ref[:, 2 * NS : BACK] = jnp.concatenate([rest[:, HEAD:], rest[:, :HEAD]], axis=1).astype(BF16)
    steps = jnp.concatenate([dt_ref[...].astype(F32), jnp.zeros((HEAD - 1, BLOCK), F32)], axis=0)
    weights_ref[:, BACK:] = jnp.concatenate([out_ref[...].astype(F32), steps], axis=0).T.astype(BF16)

    load_rows.wait()
    square = jnp.zeros((ROWS, 1), F32)
    for b in range(WIDTH // BLOCK):
        some = rows[:, b * BLOCK : (b + 1) * BLOCK].astype(F32)
        square = square + jnp.sum(some * some, axis=1, keepdims=True)
    square_ref[...] = square
    scale = lax.rsqrt(square * (1.0 / WIDTH) + 1e-05)
    for b in range(WIDTH // BLOCK):
        cols = slice(b * BLOCK, (b + 1) * BLOCK)
        rows[:, cols] = (rows[:, cols].astype(F32) * scale * gain_ref[cols].reshape(1, BLOCK)).astype(BF16)
    spans = []
    for k, ref in enumerate((h0, h1, h2, h3)):
        for b in range(4):
            block = lax.rem(train // 4 + k, NX) * 4 + (lax.rem(train, 4) ^ b)
            spans.append(
                pltpu.make_async_copy(
                    rows.at[:, pl.ds(pl.multiple_of(block * BLOCK, BLOCK), BLOCK)],
                    ref.at[:, pl.ds(b * BLOCK, BLOCK)],
                    span_sem.at[4 * k + b],
                )
            )
            spans[-1].start()
    load_states.wait()
    for o in range(N_ROLL):
        count_ref[o] = 0
    for i in range(ROWS):
        o = owner_ref[i]
        rank = count_ref[o]
        count_ref[o] = rank + 1
        place = o * CAP + rank
        place_ref[i] = place
        pltpu.make_async_copy(states.at[i], send_ref.at[place], state_sem).start()
    pltpu.make_async_copy(states, send_ref.at[pl.ds(0, ROWS)], state_sem).wait()
    for copy in spans:
        copy.wait()


def project_kernel(gain_ref, h0, h1, h2, h3, w0, w1, w2, w3, own_ref, p1, p2, p3):
    count = NX * ROWS
    total, backs = None, None
    for b, w in enumerate((w0, w1, w2, w3)):
        gain = gain_ref[b : b + 1]
        weights = w[...]
        back = weights[:, BACK:].T[:HEAD]
        gained = back.astype(F32) * gain
        high = gained.astype(BF16)
        low = (gained - high.astype(F32)).astype(BF16)
        normed = jnp.concatenate([h[:, b * BLOCK : (b + 1) * BLOCK] for h in (h0, h1, h2, h3)], axis=0)
        left = jnp.concatenate([normed, high, low], axis=0)
        part = jnp.dot(left, weights, preferred_element_type=F32)
        bare = (normed.astype(F32) * (1.0 / gain)).astype(BF16)
        left = jnp.concatenate([bare, back], axis=0)
        part_back = jnp.dot(left, weights[:, BACK:], preferred_element_type=F32)
        total = part if total is None else total + part
        backs = part_back if backs is None else backs + part_back
    total = jnp.concatenate([total[:count], total[count : count + HEAD] + total[count + HEAD :]], axis=0)
    lane = lax.broadcasted_iota(jnp.int32, backs.shape, 1)
    last = jnp.where(lane < HEAD, backs, total[:, BACK:])
    total = jnp.concatenate([total[:, :BACK], last], axis=1)
    grow = total[count:]
    own_ref[:ROWS] = total[:ROWS]
    own_ref[ROWS:] = grow
    grow_high = grow.astype(BF16)
    grow_low = (grow - grow_high.astype(F32)).astype(BF16)
    for k, ref in enumerate((p1, p2, p3)):
        rows = total[(k + 1) * ROWS : (k + 2) * ROWS]
        high = rows.astype(BF16)
        ref[:ROWS] = high
        ref[ROWS : 2 * ROWS] = (rows - high.astype(F32)).astype(BF16)
        ref[2 * ROWS : 2 * ROWS + HEAD] = grow_high
        ref[2 * ROWS + HEAD :] = grow_low


def silu(v):
    return v * jax.nn.sigmoid(v)


def decode_kernel(
    scalar_ref,
    own,
    r1,
    r2,
    r3,
    square_ref,
    state_hbm,
    conv,
    taps,
    bias,
    gain,
    code,
    placeq,
    out,
    state,
    packed,
    state_sem,
):
    load = pltpu.make_async_copy(state_hbm, state, state_sem)
    load.start()
    square = square_ref[...]
    first, grow = own[:ROWS], own[ROWS:]
    for r in (r1, r2, r3):
        first = first + (r[:ROWS].astype(F32) + r[ROWS : 2 * ROWS].astype(F32))
        grow = grow + (r[2 * ROWS : 2 * ROWS + HEAD].astype(F32) + r[2 * ROWS + HEAD :].astype(F32))
    high = grow.astype(BF16)
    grow = jnp.concatenate([high, (grow - high.astype(F32)).astype(BF16)], axis=0)
    raw = first * jnp.sqrt(square * (1.0 / WIDTH) + 1e-05)
    delta_bias, rate, skip = scalar_ref[0], jnp.exp(jnp.full((1, 1), scalar_ref[1], F32)), scalar_ref[2]
    window = [conv[k].astype(F32) for k in range(3)]
    product = jnp.ones((ROWS, 1), F32)
    scaled, inputs_b, entered = [], [], []
    row8 = lax.broadcasted_iota(jnp.int32, (8, HEAD), 0)
    for step in range(STEPS):
        if step == 0:
            projected = first
        else:
            projected = raw * lax.rsqrt(square * (1.0 / WIDTH) + 1e-05)
        conv_input = projected[:, :CONV].astype(BF16).astype(F32)
        window.append(conv_input)
        entered.append(conv_input)
        mixed = bias[...]
        for k in range(4):
            mixed = mixed + window[step + k] * taps[k : k + 1]
        mixed = silu(mixed)
        input_b, output_c, inputs_x = mixed[:, :NS], mixed[:, NS : 2 * NS], mixed[:, 2 * NS :]
        delta = jax.nn.softplus(projected[:, STEP : STEP + 1] + delta_bias)
        decay = jnp.exp(-delta * rate)
        product = product * decay
        scaled = [u * decay for u in scaled] + [delta * inputs_x]
        inputs_b.append(input_b)
        if step == STEPS - 1:
            break
        high = output_c.astype(BF16)
        low = (output_c - high.astype(F32)).astype(BF16)
        if step == 0:
            load.wait()
        reads = []
        for g in range(ROWS // 8):
            left = jnp.concatenate([high[8 * g : 8 * g + 8], low[8 * g : 8 * g + 8]], axis=0)
            acc = jnp.zeros((8, HEAD), F32)
            for half in range(2):
                four = state[8 * g + 4 * half : 8 * g + 4 * half + 4].reshape(4 * HEAD, NS)
                both = lax.dot_general(left, four, (((1,), (1,)), ((), ())), preferred_element_type=F32)
                both = both[:8] + both[8:]
                for i in range(4):
                    acc = jnp.where(row8 == 4 * half + i, both[:, HEAD * i : HEAD * (i + 1)], acc)
            reads.append(acc)
        readout = product * jnp.concatenate(reads, axis=0) + skip * inputs_x
        for u, b in zip(scaled, inputs_b):
            readout = readout + u * jnp.sum(b * output_c, axis=1, keepdims=True)
        gated = readout * silu(projected[:, GATE : GATE + HEAD])
        mean = jnp.mean(gated * gated, axis=1, keepdims=True)
        normed_out = (gated * lax.rsqrt(mean + 1e-05) * gain[...]).astype(BF16)
        twice = jnp.concatenate([normed_out, normed_out], axis=1)
        after = raw + jnp.dot(twice, grow, preferred_element_type=F32)
        cross = raw[:, BACK : BACK + HEAD] + after[:, BACK : BACK + HEAD]
        square = jnp.maximum(
            square + jnp.sum(normed_out.astype(F32) * cross, axis=1, keepdims=True), 0.0
        )
        raw = after
    lane = lax.broadcasted_iota(jnp.int32, (ROWS, CONV), 1)
    high = product.astype(BF16).astype(F32)
    entered[0] = jnp.where(
        lane == 0, code[...], jnp.where(lane == 1, high, jnp.where(lane == 2, product - high, 0.0))
    )
    for step in range(STEPS):
        packed[step * ROWS : (step + 1) * ROWS] = jnp.concatenate(
            [inputs_b[step], entered[step], scaled[step]], axis=1
        ).astype(BF16)
    picker = (
        lax.broadcasted_iota(jnp.int32, (N_ROLL * CAP * STEPS, STEPS * ROWS), 0) == placeq[...]
    ).astype(F32).astype(BF16)
    out[...] = jnp.dot(picker, packed[...], preferred_element_type=F32).astype(BF16)


def after_kernel(late, arrived, out):
    pass


def combine_kernel(
    state_hbm,
    late,
    out_hbm,
    out_conv,
    state,
    out_state,
    rows_ref,
    codes_ref,
    index_ref,
    where_ref,
    sem,
    load_sem,
    store_sem,
):
    load = pltpu.make_async_copy(state_hbm, state, load_sem)
    load.start()
    slots = N_ROLL * CAP
    pick = (lax.broadcasted_iota(jnp.int32, (8, 128), 1) == 0).astype(F32).astype(BF16)
    codes = lax.dot_general(
        pick, late[:, NS : NS + 128], (((1,), (1,)), ((), ())), preferred_element_type=F32
    ).astype(jnp.int32)
    column = lax.broadcasted_iota(jnp.int32, (8, slots * STEPS), 1)
    step_of = column % STEPS
    codes = jnp.where(step_of == 0, codes, 0)
    codes_ref[...] = codes
    copy = pltpu.make_async_copy(codes_ref, index_ref, sem)
    copy.start()
    for step in range(1, STEPS):
        codes = jnp.where(step_of == step, pltpu.roll(codes, 1, axis=1), codes)

    def spread(rows, wanted):
        return (lax.broadcasted_iota(jnp.int32, (rows, slots * STEPS), 0) == wanted[:1]).astype(F32).astype(BF16)

    by_row = jnp.where(codes > 0, (codes - 1) * STEPS + step_of, -1)
    by_step = jnp.where((codes > 0) & (step_of > 0), (step_of - 1) * ROWS + codes - 1, -1)
    rows_ref[...] = jnp.dot(spread(STEPS * ROWS, by_row), late[...], preferred_element_type=F32)
    entered = jnp.dot(
        spread((STEPS - 1) * ROWS, by_step), late[:, NS : NS + CONV], preferred_element_type=F32
    )
    entered = jnp.concatenate([entered[:, 2 * NS :], entered[:, : 2 * NS]], axis=1).astype(BF16)
    for step in range(STEPS - 1):
        out_conv[step] = entered[step * ROWS : (step + 1) * ROWS]
    copy.wait()
    for s in range(ROWS + 1):
        where_ref[s] = -1
    for k in range(slots):
        where_ref[index_ref[0, k * STEPS]] = k

    load.wait()
    stores = []
    group = 4
    lanes = group * HEAD
    some = group * STEPS
    mine = (
        lax.broadcasted_iota(jnp.int32, (some, lanes), 0) // STEPS
        == lax.broadcasted_iota(jnp.int32, (some, lanes), 1) // HEAD
    )
    for g in range(ROWS // group):
        rows = rows_ref[some * g : some * (g + 1)]
        scaled = rows[:, NS + CONV :]
        scaled = jnp.where(mine, jnp.concatenate([scaled] * group, axis=1), 0.0).astype(BF16)
        outer = lax.dot_general(
            scaled, rows[:, :NS].astype(BF16), (((0,), (0,)), ((), ())), preferred_element_type=F32
        )
        for i in range(group):
            s = group * g + i
            k = where_ref[s + 1]
            product = rows[STEPS * i : STEPS * i + 1, NS + 1 : NS + 2] + rows[STEPS * i : STEPS * i + 1, NS + 2 : NS + 3]
            kept = jnp.where(k >= 0, state[jnp.maximum(k, 0)].astype(F32), 0.0)
            out_state[s] = (kept * product + outer[HEAD * i : HEAD * (i + 1)]).astype(BF16)
        if g % 3 == 2:
            some_rows = pl.ds(group * (g - 2), 3 * group)
            stores.append(
                pltpu.make_async_copy(out_state.at[some_rows], out_hbm.at[some_rows], store_sem.at[g // 3])
            )
            stores[-1].start()
    for store in stores:
        store.wait()


def body(
    hidden,
    ssm_state,
    conv_state,
    lengths,
    dest_owner,
    dest_slot,
    weights_in,
    weights_dt,
    weights_out,
    input_gain,
    conv_weight,
    conv_bias,
    delta_bias,
    decay_log,
    skip_gain,
    output_gain,
):
    shape = jax.ShapeDtypeStruct

    states = ssm_state.reshape(ROWS, HEAD, NS)
    span = shape((ROWS, SPAN), BF16)
    send_state, place, own_weights, square, *spans = pl.pallas_call(
        prepare_kernel,
        name="prepare",
        out_shape=(
            shape((N_ROLL * CAP, HEAD, NS), BF16),
            shape((ROWS,), jnp.int32),
            shape((BLOCK, COLS), BF16),
            shape((ROWS, 1), F32),
            span,
            span,
            span,
            span,
        ),
        in_specs=[SMEM, HBM, HBM, VMEM, VMEM, VMEM, VMEM],
        out_specs=(HBM, SMEM, VMEM, VMEM, HBM, HBM, HBM, HBM),
        scratch_shapes=[
            pltpu.SMEM((N_ROLL,), jnp.int32),
            pltpu.VMEM((ROWS, HEAD, NS), BF16),
            pltpu.VMEM((ROWS, WIDTH), BF16),
            pltpu.SemaphoreType.DMA((2,)),
            pltpu.SemaphoreType.DMA,
            pltpu.SemaphoreType.DMA((4 * NX,)),
        ],
    )(
        dest_owner,
        states,
        hidden,
        input_gain,
        weights_in,
        weights_dt.reshape(1, BLOCK),
        weights_out,
    )
    got_state = lax.all_to_all(
        send_state.reshape(N_ROLL, CAP * HEAD, NS), "roll", split_axis=0, concat_axis=0, tiled=True
    )
    core_perm = [(t, t ^ 1) for t in range(16)]
    z_perm = [
        (t * N_ROLL + z * NY + y, (t ^ 2) * N_ROLL + (NZ - 1 - z) * NY + y)
        for t in range(16)
        for z in range(NZ)
        for y in range(NY)
    ]
    far = lax.ppermute(own_weights, ("train", "roll"), z_perm)
    pair = lax.ppermute(own_weights, "train", core_perm)
    far_pair = lax.ppermute(far, "train", core_perm)

    def x_perm(k):
        return [(t, (t + 4 * k) % 16) for t in range(16)]

    spans = [spans[0]] + [lax.ppermute(spans[k], "train", x_perm(k)) for k in range(1, NX)]
    train = lax.axis_index("train")
    gains = jnp.stack(
        [lax.dynamic_slice_in_dim(input_gain, (train ^ b) * BLOCK, BLOCK) for b in range(4)]
    )
    own, part1, part2, part3 = pl.pallas_call(
        project_kernel,
        name="project",
        out_shape=(shape((ROWS + HEAD, COLS), F32),) + (shape((2 * (ROWS + HEAD), COLS), BF16),) * 3,
        in_specs=[VMEM] * 9,
        out_specs=(VMEM,) * 4,
        cost_estimate=pl.CostEstimate(flops=2 * 256 * SPAN * COLS, bytes_accessed=12000000, transcendentals=0),
    )(gains, *spans, own_weights, pair, far, far_pair)
    parts = [
        lax.ppermute(part, "train", x_perm(NX - k)) for k, part in zip((1, 2, 3), (part1, part2, part3))
    ]

    conv_order = lambda v: jnp.concatenate([v[..., HEAD:], v[..., :HEAD]], axis=-1)
    code = jnp.where(lengths > STEPS, dest_slot + 1, 0).astype(F32)[:, None]
    placeq = (place[None, :] * STEPS + jnp.arange(STEPS, dtype=jnp.int32)[:, None]).reshape(1, -1)
    scalars = jnp.concatenate([delta_bias, decay_log, skip_gain])
    late = pl.pallas_call(
        decode_kernel,
        name="decode",
        out_shape=shape((N_ROLL * CAP * STEPS, LATE), BF16),
        in_specs=[SMEM] + [VMEM] * 5 + [HBM] + [VMEM] * 6,
        out_specs=VMEM,
        scratch_shapes=[
            pltpu.VMEM((ROWS, HEAD, NS), BF16),
            pltpu.VMEM((STEPS * ROWS, LATE), BF16),
            pltpu.SemaphoreType.DMA,
        ],
        cost_estimate=pl.CostEstimate(flops=26_000_000_000, bytes_accessed=40000000, transcendentals=0),
    )(
        scalars,
        own,
        *parts,
        square,
        states,
        conv_order(conv_state.transpose(1, 0, 2)),
        conv_order(conv_weight),
        conv_order(conv_bias)[None],
        output_gain[None],
        code,
        placeq,
    )
    late = pl.pallas_call(
        after_kernel,
        name="after_states",
        out_shape=shape(late.shape, BF16),
        in_specs=[HBM, HBM],
        out_specs=HBM,
        input_output_aliases={0: 0},
    )(late, got_state)
    got_late = lax.all_to_all(
        late.reshape(N_ROLL, CAP * STEPS, LATE), "roll", split_axis=0, concat_axis=0, tiled=True
    ).reshape(N_ROLL * CAP * STEPS, LATE)

    moved_state, moved_conv = pl.pallas_call(
        combine_kernel,
        name="combine",
        out_shape=(shape((ROWS, HEAD, NS), BF16), shape((3, ROWS, CONV), BF16)),
        in_specs=[HBM, VMEM],
        out_specs=(HBM, VMEM),
        scratch_shapes=[
            pltpu.VMEM((N_ROLL * CAP, HEAD, NS), BF16),
            pltpu.VMEM((ROWS, HEAD, NS), BF16),
            pltpu.VMEM((STEPS * ROWS, LATE), F32),
            pltpu.VMEM((8, N_ROLL * CAP * STEPS), jnp.int32),
            pltpu.SMEM((8, N_ROLL * CAP * STEPS), jnp.int32),
            pltpu.SMEM((ROWS + 1,), jnp.int32),
            pltpu.SemaphoreType.DMA,
            pltpu.SemaphoreType.DMA,
            pltpu.SemaphoreType.DMA((4,)),
        ],
    )(got_state.reshape(N_ROLL * CAP, HEAD, NS), got_late)
    return moved_state.reshape(ssm_state.shape), moved_conv.transpose(1, 0, 2)


def solution(mesh):
    rows = ("train", "roll")
    return jax.shard_map(
        body,
        mesh=mesh,
        in_specs=(
            P(rows, None),
            P(rows, None, None, None),
            P(rows, None, None),
            P(rows),
            P(rows),
            P(rows),
            P("train", None),
            P("train", None),
            P(None, "train"),
            P(),
            P(),
            P(),
            P(),
            P(),
            P(),
            P(),
        ),
        out_specs=(P(rows, None, None, None), P(rows, None, None)),
        check_vma=False,
    )
```

time: 321 us -> 135 us (0.42)
  the two profiles are of different devices: /device:TPU:24 before, /device:TPU:8 now
where the time goes in v1:
time: 135 us
  starting transfers between devices  45.1 us (33%)
  blocking collectives  31.6 us (23%)
  Pallas kernels  25 us (19%)
  waiting for transfers between devices  23 us (17%)
  local copies, waits for them, and re-layouts  4.38 us (3%)
  between operations  2.93 us (2%)
  other arithmetic  2.53 us (2%)
    all_to_all x1, blocking collectives, body(): lax.all_to_all(late.reshape(N_ROLL, CAP * STEPS, LATE), 'roll', split_axi...  31.6 us
    ppermute x1, waiting for transfers between devices, body(): far = lax.ppermute(own_weights, ('train', 'roll'), z_perm)  12.5 us
    ppermute x3, starting transfers between devices, body(): lax.ppermute(spans[k], 'train', x_perm(k))  11.4 us
    ppermute x1, starting transfers between devices, body(): far = lax.ppermute(own_weights, ('train', 'roll'), z_perm)  11 us
    ppermute x3, starting transfers between devices, body(): lax.ppermute(part, 'train', x_perm(NX - k))  10.2 us
    ppermute x3, waiting for transfers between devices, body(): lax.ppermute(part, 'train', x_perm(NX - k))  9.59 us
    pallas_call x1, Pallas kernels, body(): pl.pallas_call(decode_kernel, name='decode', out_shape=shape((N_ROLL * CA...  9.37 us
    all_to_all x1, starting transfers between devices, body(): lax.all_to_all(send_state.reshape(N_ROLL, CAP * HEAD, NS), 'roll', split_...  8.72 us
  transfers between devices with their start and end apart: 10, of which 4 were waited for; matrix products, arithmetic and copies ran while one was open for 4% of the time, Pallas kernels for 11%

profile of v1, /device:TPU:8, one launch (start us, length us, event | category | flops | bytes accessed | tf_op | source)
XLA Modules:
  0.0 134.5 jit_solution(15457094516907363932)
XLA Ops:
  0.6 5.2 %prepare.1 = (bf16[64,64,256]{2,1,0:T(8,128)(2,1)}, s32[48]{0:T(128)}, bf16[512,768]{1,0:T(8,128)(2,1)}, f32[48,1]{1,0:T(8,128)}, bf16[48,2048]{1,0:T(8,128)(2,1...) custom-call(s32[48]{0:T(128)} %owner_ref.1, bf16[48,64,256]{2,1,0:T(8,128)(2,1)} %bitcast.22, ...), custom_call_target="tpu_custom_call" | custom-call | tf_op jit(solution)/shard_map/prepare/pallas_call | solution.py:351
  5.9 11.0 %collective-permute-start.4 = (bf16[512,768]{1,0:T(8,128)(2,1)}, bf16[512,768]{1,0:T(8,128)(2,1)}, u32[]{:S(2)}, u32[]{:S(2)}) collective-permute-start(bf16[512,768]{1,0:T(8,128)(2,1)} %get-tuple-element.21.w0), channel_id=1, source_target_pairs={{0,88},{1,89},{2,90},{3,91},{4,92},{5,93},{6,94},{7,95},{8,80},{9,... | collective-permute-start | bytes 2359304 | tf_op jit(solution)/shard_map/ppermute | solution.py:393
  16.9 8.7 %all-to-all-start = ((bf16[32,128,256]{2,1,0:T(8,128)(2,1)}), bf16[32,128,256]{2,1,0:T(8,128)(2,1)S(1)}, u32[]{:S(2)}, u32[]{:S(2)}) async-start(bf16[32,128,256]{2,1,0:T(8,128)(2,1)} %bitcast.19), calls=%async_computation | async-start | bytes 4194304 | tf_op jit(solution)/shard_map/all_to_all | solution.py:383
  25.6 1.9 %collective-permute-start.3 = (bf16[512,768]{1,0:T(8,128)(2,1)S(1)}, bf16[512,768]{1,0:T(8,128)(2,1)}, u32[]{:S(2)}, u32[]{:S(2)}) collective-permute-start(bf16[512,768]{1,0:T(8,128)(2,1)S(1)} %copy-done.1), channel_id=1, source_target_pairs={{0,32},{32,0},{64,96},{96,64},{128,160},{160,128},{192,224},{224,1... | collective-permute-start | bytes 2359304 | tf_op jit(solution)/shard_map/ppermute | solution.py:394
  27.6 3.4 %collective-permute-start = (bf16[48,2048]{1,0:T(8,128)(2,1)}, bf16[48,2048]{1,0:T(8,128)(2,1)S(1)}, u32[]{:S(2)}, u32[]{:S(2)}) collective-permute-start(bf16[48,2048]{1,0:T(8,128)(2,1)} %get-tuple-element.18), channel_id=1, source_target_pairs={{0,128},{32,160},{64,192},{96,224},{128,256},{160,288},{192,320},{... | collective-permute-start | bytes 589832 | tf_op jit(solution)/shard_map/ppermute | solution.py:400
  31.0 4.6 %collective-permute-start.1 = (bf16[48,2048]{1,0:T(8,128)(2,1)}, bf16[48,2048]{1,0:T(8,128)(2,1)S(1)}, u32[]{:S(2)}, u32[]{:S(2)}) collective-permute-start(bf16[48,2048]{1,0:T(8,128)(2,1)} %get-tuple-element.19), channel_id=1, source_target_pairs={{0,256},{32,288},{64,320},{96,352},{128,384},{160,416},{192,448},{... | collective-permute-start | bytes 589832 | tf_op jit(solution)/shard_map/ppermute | solution.py:400
  35.6 3.4 %collective-permute-start.2 = (bf16[48,2048]{1,0:T(8,128)(2,1)}, bf16[48,2048]{1,0:T(8,128)(2,1)S(1)}, u32[]{:S(2)}, u32[]{:S(2)}) collective-permute-start(bf16[48,2048]{1,0:T(8,128)(2,1)} %get-tuple-element.20), channel_id=1, source_target_pairs={{0,384},{32,416},{64,448},{96,480},{128,0},{160,32},{192,64},{224,... | collective-permute-start | bytes 589832 | tf_op jit(solution)/shard_map/ppermute | solution.py:400
  39.0 12.5 %collective-permute-done.4.w2 = bf16[512,768]{1,0:T(8,128)(2,1)} collective-permute-done((bf16[512,768]{1,0:T(8,128)(2,1)}, bf16[512,768]{1,0:T(8,128)(2,1)}, u32[]{:S(2)}, u32[]{:S(2)}) %collective-permute-start.4) | collective-permute-done | bytes 786464 | tf_op jit(solution)/shard_map/ppermute | solution.py:393
  51.5 1.9 %collective-permute-start.5 = (bf16[512,768]{1,0:T(8,128)(2,1)}, bf16[512,768]{1,0:T(8,128)(2,1)}, u32[]{:S(2)}, u32[]{:S(2)}) collective-permute-start(bf16[512,768]{1,0:T(8,128)(2,1)} %collective-permute-done.4.w2), channel_id=1, source_target_pairs={{0,32},{32,0},{64,96},{96,64},{128,160},{160,128},{192,224},{224,1... | collective-permute-start | bytes 2359304 | tf_op jit(solution)/shard_map/ppermute | solution.py:395
  53.4 0.9 fusion.2
  54.3 0.6 pad_maximum_fusion.2.gain_ref
  55.1 0.9 collective-permute-done.5.w3
  56.0 4.8 %project.1 = (f32[112,768]{1,0:T(8,128)}, bf16[224,768]{1,0:T(8,128)(2,1)}, bf16[224,768]{1,0:T(8,128)(2,1)}, bf16[224,768]{1,0:T(8,128)(2,1)}) custom-call(f32[4,512]{1,0:T(4,128)} %pad_maximum_fusion.2.gain_ref, bf16[48,2048]{1,0:T(8,128)(2,1)} %get-tuple-element.17.h0, bf16[48,2048]{1,0:T(8,128)(2,1)} %copy-done.2, bf16[48,2048]{1,0:T(8,128)(2,1)} %copy-done.3, ...), custom_call_target="tpu_custom_call" | custom-call | flops 805306368 | bytes 12000000 | tf_op jit(solution)/shard_map/project/pallas_call | solution.py:405
  60.8 4.7 %collective-permute-start.6 = (bf16[224,768]{1,0:T(8,128)(2,1)}, bf16[224,768]{1,0:T(8,128)(2,1)S(1)}, u32[]{:S(2)}, u32[]{:S(2)}) collective-permute-start(bf16[224,768]{1,0:T(8,128)(2,1)} %get-tuple-element.23), channel_id=1, source_target_pairs={{0,384},{32,416},{64,448},{96,480},{128,0},{160,32},{192,64},{224,... | collective-permute-start | bytes 1032200 | tf_op jit(solution)/shard_map/ppermute | solution.py:414
  65.5 2.7 %collective-permute-start.7 = (bf16[224,768]{1,0:T(8,128)(2,1)}, bf16[224,768]{1,0:T(8,128)(2,1)S(1)}, u32[]{:S(2)}, u32[]{:S(2)}) collective-permute-start(bf16[224,768]{1,0:T(8,128)(2,1)} %get-tuple-element.24), channel_id=1, source_target_pairs={{0,256},{32,288},{64,320},{96,352},{128,384},{160,416},{192,448},{... | collective-permute-start | bytes 1032200 | tf_op jit(solution)/shard_map/ppermute | solution.py:414
  68.2 2.8 %collective-permute-start.8 = (bf16[224,768]{1,0:T(8,128)(2,1)}, bf16[224,768]{1,0:T(8,128)(2,1)}, u32[]{:S(2)}, u32[]{:S(2)}) collective-permute-start(bf16[224,768]{1,0:T(8,128)(2,1)} %get-tuple-element.25), channel_id=1, source_target_pairs={{0,128},{32,160},{64,192},{96,224},{128,256},{160,288},{192,320},{... | collective-permute-start | bytes 1032200 | tf_op jit(solution)/shard_map/ppermute | solution.py:414
  71.8 0.7 copy.19.code
  76.2 0.7 pad_maximum_fusion.conv
  76.9 4.0 %collective-permute-done.6.r1 = bf16[224,768]{1,0:T(8,128)(2,1)S(1)} collective-permute-done((bf16[224,768]{1,0:T(8,128)(2,1)}, bf16[224,768]{1,0:T(8,128)(2,1)S(1)}, u32[]{:S(2)}, u32[]{:S(2)}) %collective-permute-start.6) | collective-permute-done | bytes 344096 | tf_op jit(solution)/shard_map/ppermute | solution.py:414
  81.0 5.6 %collective-permute-done.8.r3 = bf16[224,768]{1,0:T(8,128)(2,1)} collective-permute-done((bf16[224,768]{1,0:T(8,128)(2,1)}, bf16[224,768]{1,0:T(8,128)(2,1)}, u32[]{:S(2)}, u32[]{:S(2)}) %collective-permute-start.8) | collective-permute-done | bytes 344096 | tf_op jit(solution)/shard_map/ppermute | solution.py:414
  86.5 9.4 %decode.1.late = bf16[256,896]{1,0:T(8,128)(2,1)} custom-call(f32[3]{0:T(128)} %pad_maximum_fusion.4.scalar_ref, f32[112,768]{1,0:T(8,128)} %get-tuple-element.22.own, bf16[224,768]{1,0:T(8,128)(2,1)} %copy-done.8, bf16[224,768]{1,0:T(8,128)(2,1)} %copy-done.9, bf16[224,768]{1,0:T(8,128)(2,1)} %collective-permute-done.8.r3, ...), custom_call_target="tpu_custom_call" | custom-call | flops 25999998976 | bytes 40000000 | tf_op jit(solution)/shard_map/decode/pallas_call | solution.py:421
  95.9 1.3 copy-done
  97.3 31.6 %all_to_all.10 = bf16[32,8,896]{2,1,0:T(8,128)(2,1)} all-to-all(bf16[32,8,896]{2,1,0:T(8,128)(2,1)} %bitcast.21), channel_id=1, replica_groups=mesh['train'=16,'roll'=32] {'roll'}, dimensions={0} | all-to-all | bytes 917504 | tf_op jit(solution)/shard_map/all_to_all | solution.py:454
  128.9 5.7 %combine.1 = (bf16[48,64,256]{2,1,0:T(8,128)(2,1)}, bf16[3,48,576]{2,1,0:T(8,128)(2,1)}) custom-call(bf16[64,64,256]{2,1,0:T(8,128)(2,1)} %bitcast.18, bf16[256,896]{1,0:T(8,128)(2,1)} %bitcast.20), custom_call_target="tpu_custom_call" | custom-call | tf_op jit(solution)/shard_map/combine/pallas_call | solution.py:458
  (48 shorter events, 2.7 us)
Async XLA Ops:
  5.9 45.6 %collective-permute-start.4 = (bf16[512,768]{1,0:T(8,128)(2,1)}, bf16[512,768]{1,0:T(8,128)(2,1)}, u32[]{:S(2)}, u32[]{:S(2)}) collective-permute-start(bf16[512,768]{1,0:T(8,128)(2,1)} %get-tuple-element.21.w0), channel_id=1, source_target_pairs={{0,88},{1,89},{2,90},{3,91},{4,92},{5,93},{6,94},{7,95},{8,80},{9,... | collective-permute-start | bytes 2359304 | tf_op jit(solution)/shard_map/ppermute | solution.py:393
  16.8 8.8 %copy-start.1 = (bf16[512,768]{1,0:T(8,128)(2,1)S(1)}, bf16[512,768]{1,0:T(8,128)(2,1)}, u32[]{:S(2)}) copy-start(bf16[512,768]{1,0:T(8,128)(2,1)} %get-tuple-element.21.w0) | copy-start | bytes 2359300
  16.8 37.4 %copy-start.7 = (f32[576]{0:T(1024)S(1)}, f32[576]{0:T(1024)}, u32[]{:S(2)}) copy-start(f32[576]{0:T(1024)} %param.27) | copy-start | bytes 6916
  16.9 38.1 %copy-start.12 = (s32[48]{0:T(128)S(1)}, s32[48]{0:T(128)}, u32[]{:S(2)}) copy-start(s32[48]{0:T(128)} %get-tuple-element.27) | copy-start | bytes 580
  16.9 38.1 %copy-start.10 = (s32[48]{0:T(128)S(1)}, s32[48]{0:T(128)}, u32[]{:S(2)}) copy-start(s32[48]{0:T(128)} %param.19) | copy-start | bytes 580
  16.9 38.1 %copy-start.11 = (s32[48]{0:T(128)S(1)}, s32[48]{0:T(128)}, u32[]{:S(2)}) copy-start(s32[48]{0:T(128)} %param.21) | copy-start | bytes 580
  16.9 79.0 %all-to-all-start = ((bf16[32,128,256]{2,1,0:T(8,128)(2,1)}), bf16[32,128,256]{2,1,0:T(8,128)(2,1)S(1)}, u32[]{:S(2)}, u32[]{:S(2)}) async-start(bf16[32,128,256]{2,1,0:T(8,128)(2,1)} %bitcast.19), calls=%async_computation | async-start | bytes 4194304 | tf_op jit(solution)/shard_map/all_to_all | solution.py:383
  25.6 45.4 %slice-start.1 = ((f32[576]{0:T(1024)}), f32[64]{0:T(128)S(1)}, s32[]{:S(2)}) async-start(f32[576]{0:T(1024)} %param.27), calls=%async_computation.3 | async-start | bytes 1024 | tf_op jit(solution)/shard_map/slice | solution.py:417
  25.6 29.4 %collective-permute-start.3 = (bf16[512,768]{1,0:T(8,128)(2,1)S(1)}, bf16[512,768]{1,0:T(8,128)(2,1)}, u32[]{:S(2)}, u32[]{:S(2)}) collective-permute-start(bf16[512,768]{1,0:T(8,128)(2,1)S(1)} %copy-done.1), channel_id=1, source_target_pairs={{0,32},{32,0},{64,96},{96,64},{128,160},{160,128},{192,224},{224,1... | collective-permute-start | bytes 2359304 | tf_op jit(solution)/shard_map/ppermute | solution.py:394
  27.6 27.4 %collective-permute-start = (bf16[48,2048]{1,0:T(8,128)(2,1)}, bf16[48,2048]{1,0:T(8,128)(2,1)S(1)}, u32[]{:S(2)}, u32[]{:S(2)}) collective-permute-start(bf16[48,2048]{1,0:T(8,128)(2,1)} %get-tuple-element.18), channel_id=1, source_target_pairs={{0,128},{32,160},{64,192},{96,224},{128,256},{160,288},{192,320},{... | collective-permute-start | bytes 589832 | tf_op jit(solution)/shard_map/ppermute | solution.py:400
  31.0 24.0 %collective-permute-start.1 = (bf16[48,2048]{1,0:T(8,128)(2,1)}, bf16[48,2048]{1,0:T(8,128)(2,1)S(1)}, u32[]{:S(2)}, u32[]{:S(2)}) collective-permute-start(bf16[48,2048]{1,0:T(8,128)(2,1)} %get-tuple-element.19), channel_id=1, source_target_pairs={{0,256},{32,288},{64,320},{96,352},{128,384},{160,416},{192,448},{... | collective-permute-start | bytes 589832 | tf_op jit(solution)/shard_map/ppermute | solution.py:400
  35.6 19.4 %collective-permute-start.2 = (bf16[48,2048]{1,0:T(8,128)(2,1)}, bf16[48,2048]{1,0:T(8,128)(2,1)S(1)}, u32[]{:S(2)}, u32[]{:S(2)}) collective-permute-start(bf16[48,2048]{1,0:T(8,128)(2,1)} %get-tuple-element.20), channel_id=1, source_target_pairs={{0,384},{32,416},{64,448},{96,480},{128,0},{160,32},{192,64},{224,... | collective-permute-start | bytes 589832 | tf_op jit(solution)/shard_map/ppermute | solution.py:400
  51.5 4.5 %collective-permute-start.5 = (bf16[512,768]{1,0:T(8,128)(2,1)}, bf16[512,768]{1,0:T(8,128)(2,1)}, u32[]{:S(2)}, u32[]{:S(2)}) collective-permute-start(bf16[512,768]{1,0:T(8,128)(2,1)} %collective-permute-done.4.w2), channel_id=1, source_target_pairs={{0,32},{32,0},{64,96},{96,64},{128,160},{160,128},{192,224},{224,1... | collective-permute-start | bytes 2359304 | tf_op jit(solution)/shard_map/ppermute | solution.py:395
  55.0 1.0 copy-start.2
  55.0 1.0 copy-start.3
  55.1 16.0 %copy-start.5 = (bf16[48,3,576]{2,0,1:T(8,128)(2,1)S(1)}, bf16[48,3,576]{2,0,1:T(8,128)(2,1)}, u32[]{:S(2)}) copy-start(bf16[48,3,576]{2,0,1:T(8,128)(2,1)} %param.18) | copy-start | bytes 497668
  56.0 15.2 %copy-start.6 = (f32[4,576]{1,0:T(4,128)S(1)}, f32[4,576]{1,0:T(4,128)}, u32[]{:S(2)}) copy-start(f32[4,576]{1,0:T(4,128)} %param.26) | copy-start | bytes 27652
  56.0 19.6 %slice-start = ((f32[4,576]{1,0:T(4,128)}), f32[4,64]{1,0:T(4,128)S(1)}, s32[]{:S(2)}) async-start(f32[4,576]{1,0:T(4,128)} %param.26), calls=%async_computation.2 | async-start | bytes 4096 | tf_op jit(solution)/shard_map/slice | solution.py:417
  60.8 20.1 %collective-permute-start.6 = (bf16[224,768]{1,0:T(8,128)(2,1)}, bf16[224,768]{1,0:T(8,128)(2,1)S(1)}, u32[]{:S(2)}, u32[]{:S(2)}) collective-permute-start(bf16[224,768]{1,0:T(8,128)(2,1)} %get-tuple-element.23), channel_id=1, source_target_pairs={{0,384},{32,416},{64,448},{96,480},{128,0},{160,32},{192,64},{224,... | collective-permute-start | bytes 1032200 | tf_op jit(solution)/shard_map/ppermute | solution.py:414
  65.5 15.5 %collective-permute-start.7 = (bf16[224,768]{1,0:T(8,128)(2,1)}, bf16[224,768]{1,0:T(8,128)(2,1)S(1)}, u32[]{:S(2)}, u32[]{:S(2)}) collective-permute-start(bf16[224,768]{1,0:T(8,128)(2,1)} %get-tuple-element.24), channel_id=1, source_target_pairs={{0,256},{32,288},{64,320},{96,352},{128,384},{160,416},{192,448},{... | collective-permute-start | bytes 1032200 | tf_op jit(solution)/shard_map/ppermute | solution.py:414
  68.2 18.3 %collective-permute-start.8 = (bf16[224,768]{1,0:T(8,128)(2,1)}, bf16[224,768]{1,0:T(8,128)(2,1)}, u32[]{:S(2)}, u32[]{:S(2)}) collective-permute-start(bf16[224,768]{1,0:T(8,128)(2,1)} %get-tuple-element.25), channel_id=1, source_target_pairs={{0,128},{32,160},{64,192},{96,224},{128,256},{160,288},{192,320},{... | collective-permute-start | bytes 1032200 | tf_op jit(solution)/shard_map/ppermute | solution.py:414
  80.9 5.6 %copy-start.8 = (bf16[224,768]{1,0:T(8,128)(2,1)}, bf16[224,768]{1,0:T(8,128)(2,1)S(1)}, u32[]{:S(2)}) copy-start(bf16[224,768]{1,0:T(8,128)(2,1)S(1)} %collective-permute-done.6.r1) | copy-start | bytes 1032196
  80.9 5.6 %copy-start.9 = (bf16[224,768]{1,0:T(8,128)(2,1)}, bf16[224,768]{1,0:T(8,128)(2,1)S(1)}, u32[]{:S(2)}) copy-start(bf16[224,768]{1,0:T(8,128)(2,1)S(1)} %collective-permute-done.7.r2) | copy-start | bytes 1032196
  95.9 1.3 %copy-start = (bf16[32,128,256]{2,1,0:T(8,128)(2,1)}, bf16[32,128,256]{2,1,0:T(8,128)(2,1)S(1)}, u32[]{:S(2)}) copy-start(bf16[32,128,256]{2,1,0:T(8,128)(2,1)S(1)} %all-to-all-done.arrived) | copy-start | bytes 6291460
  (1 other events, 1.0 us)

commit v2 on v1

--- a/solution.py
+++ b/solution.py
@@ -32,17 +32,21 @@
 HBM = pl.BlockSpec(memory_space=pltpu.HBM)
 
 
+def weights_kernel(in_ref, dt_ref, out_ref, weights_ref):
+    weights_ref[:, : 2 * NS] = in_ref[:, 2 * HEAD :]
+    rest = in_ref[:, : 2 * HEAD].astype(F32)
+    weights_ref[:, 2 * NS : BACK] = jnp.concatenate([rest[:, HEAD:], rest[:, :HEAD]], axis=1).astype(BF16)
+    steps = jnp.concatenate([dt_ref[...].astype(F32), jnp.zeros((HEAD - 1, BLOCK), F32)], axis=0)
+    weights_ref[:, BACK:] = jnp.concatenate([out_ref[...].astype(F32), steps], axis=0).T.astype(BF16)
+
+
 def prepare_kernel(
     owner_ref,
     state_ref,
     hidden_ref,
     gain_ref,
-    in_ref,
-    dt_ref,
-    out_ref,
     send_ref,
     place_ref,
-    weights_ref,
     square_ref,
     h0,
     h1,
@@ -60,12 +64,6 @@
     load_rows.start()
     load_states = pltpu.make_async_copy(state_ref, states, load_sem.at[1])
     load_states.start()
-
-    weights_ref[:, : 2 * NS] = in_ref[:, 2 * HEAD :]
-    rest = in_ref[:, : 2 * HEAD].astype(F32)
-    weights_ref[:, 2 * NS : BACK] = jnp.concatenate([rest[:, HEAD:], rest[:, :HEAD]], axis=1).astype(BF16)
-    steps = jnp.concatenate([dt_ref[...].astype(F32), jnp.zeros((HEAD - 1, BLOCK), F32)], axis=0)
-    weights_ref[:, BACK:] = jnp.concatenate([out_ref[...].astype(F32), steps], axis=0).T.astype(BF16)
 
     load_rows.wait()
     square = jnp.zeros((ROWS, 1), F32)
@@ -348,21 +346,27 @@
 
     states = ssm_state.reshape(ROWS, HEAD, NS)
     span = shape((ROWS, SPAN), BF16)
-    send_state, place, own_weights, square, *spans = pl.pallas_call(
+    own_weights = pl.pallas_call(
+        weights_kernel,
+        name="pack_weights",
+        out_shape=shape((BLOCK, COLS), BF16),
+        in_specs=[VMEM] * 3,
+        out_specs=VMEM,
+    )(weights_in, weights_dt.reshape(1, BLOCK), weights_out)
+    send_state, place, square, *spans = pl.pallas_call(
         prepare_kernel,
         name="prepare",
         out_shape=(
             shape((N_ROLL * CAP, HEAD, NS), BF16),
             shape((ROWS,), jnp.int32),
-            shape((BLOCK, COLS), BF16),
             shape((ROWS, 1), F32),
             span,
             span,
             span,
             span,
         ),
-        in_specs=[SMEM, HBM, HBM, VMEM, VMEM, VMEM, VMEM],
-        out_specs=(HBM, SMEM, VMEM, VMEM, HBM, HBM, HBM, HBM),
+        in_specs=[SMEM, HBM, HBM, VMEM],
+        out_specs=(HBM, SMEM, VMEM, HBM, HBM, HBM, HBM),
         scratch_shapes=[
             pltpu.SMEM((N_ROLL,), jnp.int32),
             pltpu.VMEM((ROWS, HEAD, NS), BF16),
@@ -376,9 +380,6 @@
         states,
         hidden,
         input_gain,
-        weights_in,
-        weights_dt.reshape(1, BLOCK),
-        weights_out,
     )
     got_state = lax.all_to_all(
         send_state.reshape(N_ROLL, CAP * HEAD, NS), "roll", split_axis=0, concat_axis=0, tiled=True

time: 135 us -> 125 us (0.926)
  blocking collectives: 31.6 us -> 24.2 us
  waiting for transfers between devices: 23 us -> 18.4 us
  Pallas kernels: 25 us -> 26.5 us
    all_to_all x1, blocking collectives: 31.6 us -> 24.2 us  [body(): lax.all_to_all(late.reshape(N_ROLL, CAP * STEPS, LATE), 'roll', split_axi...]
    ppermute x1, waiting for transfers between devices: 12.5 us -> 7.92 us  [body(): far = lax.ppermute(own_weights, ('train', 'roll'), z_perm)]
    pallas_call x0 -> x1, Pallas kernels: none -> 2.14 us  [body(): pl.pallas_call(weights_kernel, name='pack_weights', out_shape=shape((BLOC...]
  transfers between devices with their start and end apart: 10 -> 10, of which waited for: 4 -> 4; matrix products, arithmetic and copies ran while one was open for 4% -> 4% of each run, Pallas kernels for 11% -> 15%
where the time goes in v2:
time: 125 us; the launch traced here: 124 us
  starting transfers between devices  45 us (36%)
  Pallas kernels  26.5 us (21%)
  blocking collectives  24.2 us (19%)
  waiting for transfers between devices  18.4 us (15%)
  local copies, waits for them, and re-layouts  4.38 us (4%)
  between operations  2.93 us (2%)
  other arithmetic  2.53 us (2%)
    all_to_all x1, blocking collectives, body(): lax.all_to_all(late.reshape(N_ROLL, CAP * STEPS, LATE), 'roll', split_axi...  24.2 us
    ppermute x3, starting transfers between devices, body(): lax.ppermute(spans[k], 'train', x_perm(k))  11.3 us
    ppermute x1, starting transfers between devices, body(): far = lax.ppermute(own_weights, ('train', 'roll'), z_perm)  10.9 us
    ppermute x3, starting transfers between devices, body(): lax.ppermute(part, 'train', x_perm(NX - k))  10.2 us
    ppermute x3, waiting for transfers between devices, body(): lax.ppermute(part, 'train', x_perm(NX - k))  9.6 us
    pallas_call x1, Pallas kernels, body(): pl.pallas_call(decode_kernel, name='decode', out_shape=shape((N_ROLL * CA...  9.37 us
    all_to_all x1, starting transfers between devices, body(): lax.all_to_all(send_state.reshape(N_ROLL, CAP * HEAD, NS), 'roll', split_...  8.75 us
    ppermute x1, waiting for transfers between devices, body(): far = lax.ppermute(own_weights, ('train', 'roll'), z_perm)  7.92 us
  transfers between devices with their start and end apart: 10, of which 4 were waited for; matrix products, arithmetic and copies ran while one was open for 4% of the time, Pallas kernels for 15%

profile of v2, /device:TPU:8, one launch (start us, length us, event | category | flops | bytes accessed | tf_op | source)
XLA Modules:
  0.0 124.0 jit_solution(178818123519758211)
XLA Ops:
  0.6 2.1 %pack_weights.1.w0 = bf16[512,768]{1,0:T(8,128)(2,1)} custom-call(bf16[512,640]{1,0:T(8,128)(2,1)} %in_ref.1, bf16[1,512]{1,0:T(2,128)(2,1)} %bitcast.30, bf16[64,512]{1,0:T(8,128)(2,1)} %out_ref.1), custom_call_target="tpu_custom_call" | custom-call | tf_op jit(solution)/shard_map/pack_weights/pallas_call | solution.py:349
  2.8 10.9 %collective-permute-start.4 = (bf16[512,768]{1,0:T(8,128)(2,1)}, bf16[512,768]{1,0:T(8,128)(2,1)}, u32[]{:S(2)}, u32[]{:S(2)}) collective-permute-start(bf16[512,768]{1,0:T(8,128)(2,1)} %pack_weights.1.w0), channel_id=1, source_target_pairs={{0,88},{1,89},{2,90},{3,91},{4,92},{5,93},{6,94},{7,95},{8,80},{9,... | collective-permute-start | bytes 2359304 | tf_op jit(solution)/shard_map/ppermute | solution.py:394
  13.7 4.6 %prepare.1 = (bf16[64,64,256]{2,1,0:T(8,128)(2,1)}, s32[48]{0:T(128)}, f32[48,1]{1,0:T(8,128)}, bf16[48,2048]{1,0:T(8,128)(2,1)}, bf16[48,2048]{1,0:T(8,128)(2,1...) custom-call(s32[48]{0:T(128)} %owner_ref.1, bf16[48,64,256]{2,1,0:T(8,128)(2,1)} %bitcast.22, ...), custom_call_target="tpu_custom_call" | custom-call | tf_op jit(solution)/shard_map/prepare/pallas_call | solution.py:356
  18.4 8.7 %all-to-all-start = ((bf16[32,128,256]{2,1,0:T(8,128)(2,1)}), bf16[32,128,256]{2,1,0:T(8,128)(2,1)S(1)}, u32[]{:S(2)}, u32[]{:S(2)}) async-start(bf16[32,128,256]{2,1,0:T(8,128)(2,1)} %bitcast.19), calls=%async_computation | async-start | bytes 4194304 | tf_op jit(solution)/shard_map/all_to_all | solution.py:384
  27.2 1.9 %collective-permute-start.3 = (bf16[512,768]{1,0:T(8,128)(2,1)S(1)}, bf16[512,768]{1,0:T(8,128)(2,1)}, u32[]{:S(2)}, u32[]{:S(2)}) collective-permute-start(bf16[512,768]{1,0:T(8,128)(2,1)S(1)} %copy-done.1), channel_id=1, source_target_pairs={{0,32},{32,0},{64,96},{96,64},{128,160},{160,128},{192,224},{224,1... | collective-permute-start | bytes 2359304 | tf_op jit(solution)/shard_map/ppermute | solution.py:395
  29.1 3.4 %collective-permute-start = (bf16[48,2048]{1,0:T(8,128)(2,1)}, bf16[48,2048]{1,0:T(8,128)(2,1)S(1)}, u32[]{:S(2)}, u32[]{:S(2)}) collective-permute-start(bf16[48,2048]{1,0:T(8,128)(2,1)} %get-tuple-element.17), channel_id=1, source_target_pairs={{0,128},{32,160},{64,192},{96,224},{128,256},{160,288},{192,320},{... | collective-permute-start | bytes 589832 | tf_op jit(solution)/shard_map/ppermute | solution.py:401
  32.5 4.7 %collective-permute-start.1 = (bf16[48,2048]{1,0:T(8,128)(2,1)}, bf16[48,2048]{1,0:T(8,128)(2,1)S(1)}, u32[]{:S(2)}, u32[]{:S(2)}) collective-permute-start(bf16[48,2048]{1,0:T(8,128)(2,1)} %get-tuple-element.18), channel_id=1, source_target_pairs={{0,256},{32,288},{64,320},{96,352},{128,384},{160,416},{192,448},{... | collective-permute-start | bytes 589832 | tf_op jit(solution)/shard_map/ppermute | solution.py:401
  37.2 3.3 %collective-permute-start.2 = (bf16[48,2048]{1,0:T(8,128)(2,1)}, bf16[48,2048]{1,0:T(8,128)(2,1)S(1)}, u32[]{:S(2)}, u32[]{:S(2)}) collective-permute-start(bf16[48,2048]{1,0:T(8,128)(2,1)} %get-tuple-element.19), channel_id=1, source_target_pairs={{0,384},{32,416},{64,448},{96,480},{128,0},{160,32},{192,64},{224,... | collective-permute-start | bytes 589832 | tf_op jit(solution)/shard_map/ppermute | solution.py:401
  40.5 7.9 %collective-permute-done.4.w2 = bf16[512,768]{1,0:T(8,128)(2,1)} collective-permute-done((bf16[512,768]{1,0:T(8,128)(2,1)}, bf16[512,768]{1,0:T(8,128)(2,1)}, u32[]{:S(2)}, u32[]{:S(2)}) %collective-permute-start.4) | collective-permute-done | bytes 786464 | tf_op jit(solution)/shard_map/ppermute | solution.py:394
  48.4 1.9 %collective-permute-start.5 = (bf16[512,768]{1,0:T(8,128)(2,1)}, bf16[512,768]{1,0:T(8,128)(2,1)}, u32[]{:S(2)}, u32[]{:S(2)}) collective-permute-start(bf16[512,768]{1,0:T(8,128)(2,1)} %collective-permute-done.4.w2), channel_id=1, source_target_pairs={{0,32},{32,0},{64,96},{96,64},{128,160},{160,128},{192,224},{224,1... | collective-permute-start | bytes 2359304 | tf_op jit(solution)/shard_map/ppermute | solution.py:396
  50.3 0.9 fusion.2
  52.0 0.9 collective-permute-done.5.w3
  52.9 4.8 %project.1 = (f32[112,768]{1,0:T(8,128)}, bf16[224,768]{1,0:T(8,128)(2,1)}, bf16[224,768]{1,0:T(8,128)(2,1)}, bf16[224,768]{1,0:T(8,128)(2,1)}) custom-call(f32[4,512]{1,0:T(4,128)} %pad_maximum_fusion.2.gain_ref, bf16[48,2048]{1,0:T(8,128)(2,1)} %get-tuple-element.16.h0, bf16[48,2048]{1,0:T(8,128)(2,1)} %copy-done.2, bf16[48,2048]{1,0:T(8,128)(2,1)} %copy-done.3, ...), custom_call_target="tpu_custom_call" | custom-call | flops 805306368 | bytes 12000000 | tf_op jit(solution)/shard_map/project/pallas_call | solution.py:406
  57.7 4.7 %collective-permute-start.6 = (bf16[224,768]{1,0:T(8,128)(2,1)}, bf16[224,768]{1,0:T(8,128)(2,1)S(1)}, u32[]{:S(2)}, u32[]{:S(2)}) collective-permute-start(bf16[224,768]{1,0:T(8,128)(2,1)} %get-tuple-element.21), channel_id=1, source_target_pairs={{0,384},{32,416},{64,448},{96,480},{128,0},{160,32},{192,64},{224,... | collective-permute-start | bytes 1032200 | tf_op jit(solution)/shard_map/ppermute | solution.py:415
  62.4 2.7 %collective-permute-start.7 = (bf16[224,768]{1,0:T(8,128)(2,1)}, bf16[224,768]{1,0:T(8,128)(2,1)S(1)}, u32[]{:S(2)}, u32[]{:S(2)}) collective-permute-start(bf16[224,768]{1,0:T(8,128)(2,1)} %get-tuple-element.22), channel_id=1, source_target_pairs={{0,256},{32,288},{64,320},{96,352},{128,384},{160,416},{192,448},{... | collective-permute-start | bytes 1032200 | tf_op jit(solution)/shard_map/ppermute | solution.py:415
  65.1 2.8 %collective-permute-start.8 = (bf16[224,768]{1,0:T(8,128)(2,1)}, bf16[224,768]{1,0:T(8,128)(2,1)}, u32[]{:S(2)}, u32[]{:S(2)}) collective-permute-start(bf16[224,768]{1,0:T(8,128)(2,1)} %get-tuple-element.23), channel_id=1, source_target_pairs={{0,128},{32,160},{64,192},{96,224},{128,256},{160,288},{192,320},{... | collective-permute-start | bytes 1032200 | tf_op jit(solution)/shard_map/ppermute | solution.py:415
  68.8 0.7 copy.19.code
  73.2 0.7 pad_maximum_fusion.conv
  73.8 4.0 %collective-permute-done.6.r1 = bf16[224,768]{1,0:T(8,128)(2,1)S(1)} collective-permute-done((bf16[224,768]{1,0:T(8,128)(2,1)}, bf16[224,768]{1,0:T(8,128)(2,1)S(1)}, u32[]{:S(2)}, u32[]{:S(2)}) %collective-permute-start.6) | collective-permute-done | bytes 344096 | tf_op jit(solution)/shard_map/ppermute | solution.py:415
  77.9 5.6 %collective-permute-done.8.r3 = bf16[224,768]{1,0:T(8,128)(2,1)} collective-permute-done((bf16[224,768]{1,0:T(8,128)(2,1)}, bf16[224,768]{1,0:T(8,128)(2,1)}, u32[]{:S(2)}, u32[]{:S(2)}) %collective-permute-start.8) | collective-permute-done | bytes 344096 | tf_op jit(solution)/shard_map/ppermute | solution.py:415
  83.5 9.4 %decode.1.late = bf16[256,896]{1,0:T(8,128)(2,1)} custom-call(f32[3]{0:T(128)} %pad_maximum_fusion.4.scalar_ref, f32[112,768]{1,0:T(8,128)} %get-tuple-element.20.own, bf16[224,768]{1,0:T(8,128)(2,1)} %copy-done.8, bf16[224,768]{1,0:T(8,128)(2,1)} %copy-done.9, bf16[224,768]{1,0:T(8,128)(2,1)} %collective-permute-done.8.r3, ...), custom_call_target="tpu_custom_call" | custom-call | flops 25999998976 | bytes 40000000 | tf_op jit(solution)/shard_map/decode/pallas_call | solution.py:422
  92.9 1.3 %copy-done = bf16[32,128,256]{2,1,0:T(8,128)(2,1)} copy-done((bf16[32,128,256]{2,1,0:T(8,128)(2,1)}, bf16[32,128,256]{2,1,0:T(8,128)(2,1)S(1)}, u32[]{:S(2)}) %copy-start) | copy-done | bytes 2097176
  94.2 24.2 %all_to_all.10 = bf16[32,8,896]{2,1,0:T(8,128)(2,1)} all-to-all(bf16[32,8,896]{2,1,0:T(8,128)(2,1)} %bitcast.21), channel_id=1, replica_groups=mesh['train'=16,'roll'=32] {'roll'}, dimensions={0} | all-to-all | bytes 917504 | tf_op jit(solution)/shard_map/all_to_all | solution.py:455
  118.4 5.7 %combine.1 = (bf16[48,64,256]{2,1,0:T(8,128)(2,1)}, bf16[3,48,576]{2,1,0:T(8,128)(2,1)}) custom-call(bf16[64,64,256]{2,1,0:T(8,128)(2,1)} %bitcast.18, bf16[256,896]{1,0:T(8,128)(2,1)} %bitcast.20), custom_call_target="tpu_custom_call" | custom-call | tf_op jit(solution)/shard_map/combine/pallas_call | solution.py:459
  (49 shorter events, 3.4 us)
Async XLA Ops:
  2.8 45.6 %collective-permute-start.4 = (bf16[512,768]{1,0:T(8,128)(2,1)}, bf16[512,768]{1,0:T(8,128)(2,1)}, u32[]{:S(2)}, u32[]{:S(2)}) collective-permute-start(bf16[512,768]{1,0:T(8,128)(2,1)} %pack_weights.1.w0), channel_id=1, source_target_pairs={{0,88},{1,89},{2,90},{3,91},{4,92},{5,93},{6,94},{7,95},{8,80},{9,... | collective-permute-start | bytes 2359304 | tf_op jit(solution)/shard_map/ppermute | solution.py:394
  18.3 8.8 %copy-start.1 = (bf16[512,768]{1,0:T(8,128)(2,1)S(1)}, bf16[512,768]{1,0:T(8,128)(2,1)}, u32[]{:S(2)}) copy-start(bf16[512,768]{1,0:T(8,128)(2,1)} %pack_weights.1.w0) | copy-start | bytes 2359300
  18.3 32.9 %copy-start.7 = (f32[576]{0:T(1024)S(1)}, f32[576]{0:T(1024)}, u32[]{:S(2)}) copy-start(f32[576]{0:T(1024)} %param.27) | copy-start | bytes 6916
  18.4 33.5 %copy-start.12 = (s32[48]{0:T(128)S(1)}, s32[48]{0:T(128)}, u32[]{:S(2)}) copy-start(s32[48]{0:T(128)} %get-tuple-element.25) | copy-start | bytes 580
  18.4 33.5 %copy-start.10 = (s32[48]{0:T(128)S(1)}, s32[48]{0:T(128)}, u32[]{:S(2)}) copy-start(s32[48]{0:T(128)} %param.19) | copy-start | bytes 580
  18.4 33.5 %copy-start.11 = (s32[48]{0:T(128)S(1)}, s32[48]{0:T(128)}, u32[]{:S(2)}) copy-start(s32[48]{0:T(128)} %param.21) | copy-start | bytes 580
  18.4 74.5 %all-to-all-start = ((bf16[32,128,256]{2,1,0:T(8,128)(2,1)}), bf16[32,128,256]{2,1,0:T(8,128)(2,1)S(1)}, u32[]{:S(2)}, u32[]{:S(2)}) async-start(bf16[32,128,256]{2,1,0:T(8,128)(2,1)} %bitcast.19), calls=%async_computation | async-start | bytes 4194304 | tf_op jit(solution)/shard_map/all_to_all | solution.py:384
  27.1 40.8 %slice-start.1 = ((f32[576]{0:T(1024)}), f32[64]{0:T(128)S(1)}, s32[]{:S(2)}) async-start(f32[576]{0:T(1024)} %param.27), calls=%async_computation.3 | async-start | bytes 1024 | tf_op jit(solution)/shard_map/slice | solution.py:418
  27.2 24.8 %collective-permute-start.3 = (bf16[512,768]{1,0:T(8,128)(2,1)S(1)}, bf16[512,768]{1,0:T(8,128)(2,1)}, u32[]{:S(2)}, u32[]{:S(2)}) collective-permute-start(bf16[512,768]{1,0:T(8,128)(2,1)S(1)} %copy-done.1), channel_id=1, source_target_pairs={{0,32},{32,0},{64,96},{96,64},{128,160},{160,128},{192,224},{224,1... | collective-permute-start | bytes 2359304 | tf_op jit(solution)/shard_map/ppermute | solution.py:395
  29.1 22.8 %collective-permute-start = (bf16[48,2048]{1,0:T(8,128)(2,1)}, bf16[48,2048]{1,0:T(8,128)(2,1)S(1)}, u32[]{:S(2)}, u32[]{:S(2)}) collective-permute-start(bf16[48,2048]{1,0:T(8,128)(2,1)} %get-tuple-element.17), channel_id=1, source_target_pairs={{0,128},{32,160},{64,192},{96,224},{128,256},{160,288},{192,320},{... | collective-permute-start | bytes 589832 | tf_op jit(solution)/shard_map/ppermute | solution.py:401
  32.5 19.5 %collective-permute-start.1 = (bf16[48,2048]{1,0:T(8,128)(2,1)}, bf16[48,2048]{1,0:T(8,128)(2,1)S(1)}, u32[]{:S(2)}, u32[]{:S(2)}) collective-permute-start(bf16[48,2048]{1,0:T(8,128)(2,1)} %get-tuple-element.18), channel_id=1, source_target_pairs={{0,256},{32,288},{64,320},{96,352},{128,384},{160,416},{192,448},{... | collective-permute-start | bytes 589832 | tf_op jit(solution)/shard_map/ppermute | solution.py:401
  37.2 14.8 %collective-permute-start.2 = (bf16[48,2048]{1,0:T(8,128)(2,1)}, bf16[48,2048]{1,0:T(8,128)(2,1)S(1)}, u32[]{:S(2)}, u32[]{:S(2)}) collective-permute-start(bf16[48,2048]{1,0:T(8,128)(2,1)} %get-tuple-element.19), channel_id=1, source_target_pairs={{0,384},{32,416},{64,448},{96,480},{128,0},{160,32},{192,64},{224,... | collective-permute-start | bytes 589832 | tf_op jit(solution)/shard_map/ppermute | solution.py:401
  48.4 4.5 %collective-permute-start.5 = (bf16[512,768]{1,0:T(8,128)(2,1)}, bf16[512,768]{1,0:T(8,128)(2,1)}, u32[]{:S(2)}, u32[]{:S(2)}) collective-permute-start(bf16[512,768]{1,0:T(8,128)(2,1)} %collective-permute-done.4.w2), channel_id=1, source_target_pairs={{0,32},{32,0},{64,96},{96,64},{128,160},{160,128},{192,224},{224,1... | collective-permute-start | bytes 2359304 | tf_op jit(solution)/shard_map/ppermute | solution.py:396
  51.9 1.0 copy-start.2
  52.0 1.0 copy-start.3
  52.0 15.9 %copy-start.5 = (bf16[48,3,576]{2,0,1:T(8,128)(2,1)S(1)}, bf16[48,3,576]{2,0,1:T(8,128)(2,1)}, u32[]{:S(2)}) copy-start(bf16[48,3,576]{2,0,1:T(8,128)(2,1)} %param.18) | copy-start | bytes 497668
  52.9 15.1 %copy-start.6 = (f32[4,576]{1,0:T(4,128)S(1)}, f32[4,576]{1,0:T(4,128)}, u32[]{:S(2)}) copy-start(f32[4,576]{1,0:T(4,128)} %param.26) | copy-start | bytes 27652
  52.9 19.6 %slice-start = ((f32[4,576]{1,0:T(4,128)}), f32[4,64]{1,0:T(4,128)S(1)}, s32[]{:S(2)}) async-start(f32[4,576]{1,0:T(4,128)} %param.26), calls=%async_computation.2 | async-start | bytes 4096 | tf_op jit(solution)/shard_map/slice | solution.py:418
  57.7 20.1 %collective-permute-start.6 = (bf16[224,768]{1,0:T(8,128)(2,1)}, bf16[224,768]{1,0:T(8,128)(2,1)S(1)}, u32[]{:S(2)}, u32[]{:S(2)}) collective-permute-start(bf16[224,768]{1,0:T(8,128)(2,1)} %get-tuple-element.21), channel_id=1, source_target_pairs={{0,384},{32,416},{64,448},{96,480},{128,0},{160,32},{192,64},{224,... | collective-permute-start | bytes 1032200 | tf_op jit(solution)/shard_map/ppermute | solution.py:415
  62.4 15.5 %collective-permute-start.7 = (bf16[224,768]{1,0:T(8,128)(2,1)}, bf16[224,768]{1,0:T(8,128)(2,1)S(1)}, u32[]{:S(2)}, u32[]{:S(2)}) collective-permute-start(bf16[224,768]{1,0:T(8,128)(2,1)} %get-tuple-element.22), channel_id=1, source_target_pairs={{0,256},{32,288},{64,320},{96,352},{128,384},{160,416},{192,448},{... | collective-permute-start | bytes 1032200 | tf_op jit(solution)/shard_map/ppermute | solution.py:415
  65.1 18.4 %collective-permute-start.8 = (bf16[224,768]{1,0:T(8,128)(2,1)}, bf16[224,768]{1,0:T(8,128)(2,1)}, u32[]{:S(2)}, u32[]{:S(2)}) collective-permute-start(bf16[224,768]{1,0:T(8,128)(2,1)} %get-tuple-element.23), channel_id=1, source_target_pairs={{0,128},{32,160},{64,192},{96,224},{128,256},{160,288},{192,320},{... | collective-permute-start | bytes 1032200 | tf_op jit(solution)/shard_map/ppermute | solution.py:415
  77.9 5.6 %copy-start.8 = (bf16[224,768]{1,0:T(8,128)(2,1)}, bf16[224,768]{1,0:T(8,128)(2,1)S(1)}, u32[]{:S(2)}) copy-start(bf16[224,768]{1,0:T(8,128)(2,1)S(1)} %collective-permute-done.6.r1) | copy-start | bytes 1032196
  77.9 5.6 %copy-start.9 = (bf16[224,768]{1,0:T(8,128)(2,1)}, bf16[224,768]{1,0:T(8,128)(2,1)S(1)}, u32[]{:S(2)}) copy-start(bf16[224,768]{1,0:T(8,128)(2,1)S(1)} %collective-permute-done.7.r2) | copy-start | bytes 1032196
  92.8 1.3 %copy-start = (bf16[32,128,256]{2,1,0:T(8,128)(2,1)}, bf16[32,128,256]{2,1,0:T(8,128)(2,1)S(1)}, u32[]{:S(2)}) copy-start(bf16[32,128,256]{2,1,0:T(8,128)(2,1)S(1)} %all-to-all-done.arrived) | copy-start | bytes 6291460
  (1 other events, 0.9 us)
